TPU v7x, 32 devices: a whole 2x2x4 slice. The times are simulated.
32 devices in a mesh: dp: 4 (over y, core), expert: 8 (over z, x).
Axes of the slice: x: 2, y: 2, z: 4, core: 2. Of those that a mesh axis runs over, the one named last changes fastest.
Arguments:
- hidden_token_tiles: bfloat16 [4, 512, 1024], P(None, 'dp'), may hold values from -6 to 6
- gradient_token_tiles: bfloat16 [4, 7168, 512], P(None, 'expert', 'dp'), may hold values from -0.59765625 to 0.59765625
- momentum: float32 [4, 7168, 1024], P('dp', 'expert'), may hold values from -54 to 54, as said below
- filled_tile_count: int32 [4, 4], replicated, may hold values from 1 to 8, as said below
Outputs:
- new_momentum: float32 [4, 7168, 1024], P('dp', 'expert')
- update: float32 [4, 7168, 1024], P(None, 'expert')
Inputs may be any that keep to these rules, and one draw needn't show every extreme that they name: momentum entries are finite reals. filled_tile_count[g, x] filled tiles stand at the head of group g's slots for expert x; in every draw one expert is full in every group.
All inputs are finite; a program needn't handle non-finite values.
Results may differ from a plain program's by a relative error of at most 0.0009.
Values may be sent and summed in bfloat16 or wider, within the bound.
A program may use at most 128 MiB of HBM per device.

v0:
```python
import math

import jax
import jax.numpy as jnp
from jax import lax
from jax.sharding import PartitionSpec as P

D = 7168
FF = 1024
TILE = 16
ITERS = 2


MOMENTUM_DECAY = 0.95
EPSILON = 1e-07
COEF_A = 3.4445
COEF_B = -4.775
COEF_C = 2.0315


def full_dot(left, right):
    return jnp.dot(left, right, precision=lax.Precision.HIGHEST, preferred_element_type=jnp.float32)


def body(hidden_token_tiles, gradient_token_tiles, momentum, filled_tile_count):
    group = lax.axis_index("dp")
    rows_group = hidden_token_tiles.shape[1]
    experts_here = hidden_token_tiles.shape[0]
    limits = lax.dynamic_index_in_dim(filled_tile_count, group, 0, keepdims=False) * TILE
    positions = lax.broadcasted_iota(jnp.int32, (experts_here, rows_group), 1)
    tallied_tiles = positions < limits[:, None]
    retained_entries = jnp.where(
        tallied_tiles[:, :, None], hidden_token_tiles, jnp.zeros((), jnp.bfloat16)
    )
    gradient = lax.psum_scatter(
        jnp.einsum(
            "tba,tan->tbn",
            gradient_token_tiles,
            retained_entries,
            preferred_element_type=jnp.float32,
        ),
        "dp",
        scatter_dimension=0,
        tiled=True,
    )[0]
    moment = MOMENTUM_DECAY * momentum[0] + gradient
    current = moment
    for iteration in range(ITERS):
        gram_total = lax.psum(full_dot(current.T, current).astype(jnp.bfloat16), "expert").astype(
            jnp.float32
        )
        if iteration == 0:
            factor = 1.0 / (jnp.sqrt(jnp.trace(gram_total)) + EPSILON)
            current = current * factor
            gram_total = gram_total * (factor * factor)
        mixer = COEF_B * gram_total + COEF_C * full_dot(gram_total, gram_total)
        current = COEF_A * current + full_dot(current, mixer)
    update_local = current * math.sqrt(max(FF, D))
    gathered = lax.all_gather(update_local[None], "dp", axis=0, tiled=True)
    return (moment[None], gathered)


def solution(mesh):
    placed = (P(None, "dp", None), P(None, "expert", "dp"), P("dp", "expert", None), P())
    return jax.shard_map(
        body,
        mesh=mesh,
        in_specs=placed,
        out_specs=(P("dp", "expert", None), P(None, "expert", None)),
        check_vma=False,
    )
```

profile of v0, /device:TPU:0, one launch (start us, length us, event | category | flops | bytes accessed | tf_op | source)
XLA Modules:
  0.0 544.5 jit_solution(672301994801470890)
XLA Ops:
  7.2 0.0 copy-start
  7.2 0.0 reduce-scatter.2.cloned.1.call-start
  7.2 0.8 multiply_bitcast_fusion
  8.0 0.1 iota_compare_fusion.1
  8.1 0.3 copy-done
  8.4 8.9 %convolution_bitcast_fusion = f32[4,896,1024]{1,2,0:T(8,128)} fusion(bf16[4,896,128]{2,1,0:T(8,128)(2,1)S(1)} %copy-done, bf16[4,128,1024]{2,1,0:T(8,128)(2,1)} %param.4, pred[4,128]{1,0:T(4,128)(4,1)S(1)} %iota_compare_fusion.1), kind=kOutput, calls=%fused_computation | convolution fusion | flops 940048384 | bytes 16646656 | tf_op jit(solution)/shard_map/tba,tan->tbn/dot_general | solution.py:36
  17.3 0.0 reduce-scatter.2.cloned.1.call-update
  17.3 0.0 all-reduce.3.cloned.1.call-start
  17.4 5.0 copy.6
  22.4 110.7 %reduce-scatter.2.cloned.1.call-done = f32[1,896,1024]{1,2,0:T(8,128)} async-done(((f32[4,896,1024]{1,2,0:T(8,128)}), f32[1,896,1024]{1,2,0:T(8,128)}) %reduce-scatter.2.cloned.1.call-update) | async-done | bytes 3670032 | tf_op jit(solution)/shard_map/reduce_scatter | solution.py:35
  133.2 3.6 multiply_add_fusion
  136.7 0.0 copy-start.2
  136.7 1.8 copy-done.2
  138.6 14.4 %fusion.29 = bf16[1024,1024]{1,0:T(8,128)(2,1)} fusion(f32[1,896,1024]{1,2,0:T(8,128)S(1)} %multiply_add_fusion), kind=kOutput, calls=%fused_computation.29 | convolution fusion | flops 11275337728 | bytes 5767168 | tf_op jit(solution)/shard_map/dot_general | solution.py:22
  152.9 0.0 all-reduce.3.cloned.1.call-update
  153.0 0.2 all-reduce.5.cloned.1.call-start
  153.2 101.8 %all-reduce.3.cloned.1.call-done = bf16[1024,1024]{1,0:T(8,128)(2,1)} async-done(((bf16[1024,1024]{1,0:T(8,128)(2,1)}), bf16[1024,1024]{1,0:T(8,128)(2,1)}) %all-reduce.3.cloned.1.call-update) | async-done | bytes 2097168 | tf_op jit(solution)/shard_map/psum | solution.py:49
  254.9 2.3 fusion.5
  258.0 0.0 copy-start.3
  258.0 16.2 %fusion = f32[1024,1024]{1,0:T(8,128)S(1)} fusion(bf16[1024,1024]{1,0:T(8,128)(2,1)} %all-reduce.3.cloned.1.call-done, f32[]{:T(128)S(6)} %mul.70), kind=kOutput, calls=%fused_computation.3 | convolution fusion | flops 12886999040 | bytes 6291460 | tf_op jit(solution)/shard_map/dot_general | solution.py:22
  274.3 15.5 %fusion.13 = f32[896,1024]{0,1:T(8,128)S(1)} fusion(f32[1,896,1024]{1,2,0:T(8,128)S(1)} %copy-done.3, bf16[1024,1024]{1,0:T(8,128)(2,1)S(1)} %copy-done.4, f32[1024,1024]{1,0:T(8,128)S(1)} %fusion, f32[]{:T(128)S(6)} %mul.70, f32[]{:T(128)S(6)} %div.3), kind=kOutput, calls=%fused_computation.17 | convolution fusion | flops 11283202048 | bytes 13631496 | tf_op jit(solution)/shard_map/dot_general | solution.py:22
  289.8 1.8 copy-done.6
  291.6 14.4 %convolution_convert_fusion = bf16[1024,1024]{1,0:T(8,128)(2,1)} fusion(f32[896,1024]{0,1:T(8,128)S(1)} %fusion.13), kind=kOutput, calls=%fused_computation.30 | convolution fusion | flops 11275337728 | bytes 5767168 | tf_op jit(solution)/shard_map/dot_general | solution.py:22
  306.0 0.0 all-reduce.5.cloned.1.call-update
  306.0 0.2 all-gather.3.cloned.1.call-start
  306.3 101.4 %all-reduce.5.cloned.1.call-done = bf16[1024,1024]{1,0:T(8,128)(2,1)} async-done(((bf16[1024,1024]{1,0:T(8,128)(2,1)}), bf16[1024,1024]{1,0:T(8,128)(2,1)}) %all-reduce.5.cloned.1.call-update) | async-done | bytes 2097168 | tf_op jit(solution)/shard_map/psum | solution.py:49
  407.7 4.7 fusion.41
  412.4 16.0 %add_multiply_fusion = f32[896,1024]{0,1:T(8,128)} fusion(f32[896,1024]{0,1:T(8,128)S(1)} %copy-done.7, f32[1024,1024]{1,0:T(8,128)S(1)} %fusion.41, bf16[1024,1024]{1,0:T(8,128)(2,1)S(1)} %copy-done.5), kind=kOutput, calls=%fused_computation.20 | convolution fusion | flops 11281235968 | bytes 13631488 | tf_op jit(solution)/shard_map/dot_general | solution.py:22
  428.4 0.0 all-gather.3.cloned.1.call-update
  428.4 5.0 copy.10
  433.4 88.9 %all-gather.3.cloned.1.call-done = f32[3584,1024]{0,1:T(8,128)} async-done(((f32[896,1024]{0,1:T(8,128)}), f32[3584,1024]{0,1:T(8,128)}) %all-gather.3.cloned.1.call-update) | async-done | bytes 14680080 | tf_op jit(solution)/shard_map/all_gather | solution.py:59
  522.4 15.4 %copy.15 = f32[3584,1024]{1,0:T(8,128)} copy(f32[3584,1024]{0,1:T(8,128)} %all-gather.3.cloned.1.call-done) | data formatting | bytes 29360128
  (10 shorter events, 0.0 us)
Async XLA Ops:
  7.2 1.2 copy-start
  7.2 126.0 %reduce-scatter.2.cloned.1.call-start = ((), (), s32[]{:S(2)}) async-start(), calls=%async_computation.1 | async-start | bytes 18350080 | tf_op jit(solution)/shard_map/reduce_scatter | solution.py:35
  17.3 237.6 %all-reduce.3.cloned.1.call-start = ((), (), s32[]{:S(2)}) async-start(), calls=%async_computation.2 | async-start | bytes 4194304 | tf_op jit(solution)/shard_map/psum | solution.py:49
  136.7 1.8 copy-start.2
  153.0 254.7 %all-reduce.5.cloned.1.call-start = ((), (), s32[]{:S(2)}) async-start(), calls=%async_computation.3 | async-start | bytes 4194304 | tf_op jit(solution)/shard_map/psum | solution.py:49
  258.0 16.3 %copy-start.3 = (f32[1,896,1024]{1,2,0:T(8,128)S(1)}, f32[1,896,1024]{1,2,0:T(8,128)}, u32[]{:S(2)}) copy-start(f32[1,896,1024]{1,2,0:T(8,128)} %copy-done.2) | copy-start | bytes 11010052
  258.0 16.3 %copy-start.4 = (bf16[1024,1024]{1,0:T(8,128)(2,1)S(1)}, bf16[1024,1024]{1,0:T(8,128)(2,1)}, u32[]{:S(2)}) copy-start(bf16[1024,1024]{1,0:T(8,128)(2,1)} %all-reduce.3.cloned.1.call-done) | copy-start | bytes 6291460
  289.8 1.8 copy-start.6
  306.0 216.3 %all-gather.3.cloned.1.call-start = ((), (), s32[]{:S(2)}) async-start(), calls=%async_computation.4 | async-start | bytes 18350080 | tf_op jit(solution)/shard_map/all_gather | solution.py:59
  407.7 4.7 copy-start.5
  407.7 4.7 copy-start.7
  522.3 15.4 %copy-start.1 = (bf16[4,896,128]{2,1,0:T(8,128)(2,1)S(1)}, bf16[4,896,128]{2,1,0:T(8,128)(2,1)}, u32[]{:S(2)}) copy-start(bf16[4,896,128]{2,1,0:T(8,128)(2,1)} %param.5) | copy-start | bytes 2752516
Sparse Core Ops, SparseCore 0:
  17.5 115.6 reduce-scatter.1
  153.1 101.8 all-reduce.2
  306.2 101.4 all-reduce.4
  428.6 93.7 all-gather.2
where the time goes:
time: 552 us; the launch traced here: 544 us
  waiting for transfers between devices  403 us (73%)
  matrix products  90.1 us (16%)
  local copies, waits for them, and re-layouts  29.4 us (5%)
  between operations  14.8 us (3%)
  other arithmetic  6.74 us (1%)
    psum x2, waiting for transfers between devices, body(): lax.psum(full_dot(current.T, current).astype(jnp.bfloat16), 'expert')  203 us
    reduce_scatter x1, waiting for transfers between devices, body(): lax.psum_scatter(jnp.einsum('tba,tan->tbn', gradient_token_tiles, retaine...  111 us
    all_gather x1, waiting for transfers between devices, body(): gathered = lax.all_gather(update_local[None], 'dp', axis=0, tiled=True)  88.9 us
    dot_general x6, matrix products, full_dot(): jnp.dot(left, right, precision=lax.Precision.HIGHEST, preferred_element_t...  81.2 us
    unnamed x19, local copies, waits for them, and re-layouts  29.4 us
  transfers between devices with their start and end apart: 4, of which 4 were waited for; matrix products, arithmetic and copies ran while one was open for 2% of the time, Pallas kernels for 0%

commit v1 on v0

v1 whole, which is shorter than its diff:
```python
import math

import jax
import jax.numpy as jnp
from jax import lax
from jax.sharding import PartitionSpec as P

D = 7168
FF = 1024
TILE = 16
ITERS = 2


MOMENTUM_DECAY = 0.95
EPSILON = 1e-07
COEF_A = 3.4445
COEF_B = -4.775
COEF_C = 2.0315

BF16 = jnp.bfloat16


def dot16(left, right):
    return jnp.dot(left.astype(BF16), right.astype(BF16), preferred_element_type=jnp.float32)


def split16(array):
    high = array.astype(BF16)
    return high, (array - high.astype(jnp.float32)).astype(BF16)


def gram_of(moment):
    high, low = split16(moment)
    cross = jnp.dot(high.T, low, preferred_element_type=jnp.float32)
    return jnp.dot(high.T, high, preferred_element_type=jnp.float32) + cross + cross.T


def mixers(gram):
    first = COEF_B * gram + COEF_C * dot16(gram, gram)
    square = 2.0 * COEF_A * first + dot16(first, first)
    gram_next = COEF_A * COEF_A * gram + dot16(gram, square)
    second = COEF_B * gram_next + COEF_C * dot16(gram_next, gram_next)
    return COEF_A * (first + second) + dot16(first, second)


def body(hidden_token_tiles, gradient_token_tiles, momentum, filled_tile_count):
    group = lax.axis_index("dp")
    rows_group = hidden_token_tiles.shape[1]
    experts_here = hidden_token_tiles.shape[0]
    limits = lax.dynamic_index_in_dim(filled_tile_count, group, 0, keepdims=False) * TILE
    positions = lax.broadcasted_iota(jnp.int32, (experts_here, rows_group), 1)
    tallied_tiles = positions < limits[:, None]
    retained_entries = jnp.where(
        tallied_tiles[:, :, None], hidden_token_tiles, jnp.zeros((), jnp.bfloat16)
    )
    rows_all = lax.all_to_all(retained_entries, "dp", 0, 1, tiled=True)[0]
    columns_all = lax.all_to_all(gradient_token_tiles, "dp", 0, 2, tiled=True)[0]
    gradient = jnp.dot(columns_all, rows_all, preferred_element_type=jnp.float32)
    moment = MOMENTUM_DECAY * momentum[0] + gradient
    gram_total = lax.psum(gram_of(moment).astype(BF16), "expert").astype(jnp.float32)
    factor = 1.0 / (jnp.sqrt(jnp.trace(gram_total)) + EPSILON)
    current = moment * factor
    mixer = mixers(gram_total * (factor * factor))
    current = COEF_A * COEF_A * current + jnp.dot(
        current, mixer, precision=lax.Precision.HIGH, preferred_element_type=jnp.float32
    )
    update_local = current * math.sqrt(max(FF, D))
    gathered = lax.all_gather(update_local.astype(jnp.float16)[None], "dp", axis=0, tiled=True)
    return (moment[None], gathered.astype(jnp.float32))


def solution(mesh):
    placed = (P(None, "dp", None), P(None, "expert", "dp"), P("dp", "expert", None), P())
    return jax.shard_map(
        body,
        mesh=mesh,
        in_specs=placed,
        out_specs=(P("dp", "expert", None), P(None, "expert", None)),
        check_vma=False,
    )
```

time: 552 us -> 286 us (0.52); the launches traced: 544 us -> 285 us
  waiting for transfers between devices: 403 us -> 118 us
  blocking collectives: 0 us -> 44.3 us
  matrix products: 90.1 us -> 53.8 us
  starting transfers between devices: 0.51 us -> 7.8 us
    reduce_scatter x1 -> x0, waiting for transfers between devices: 111 us -> none  [body(): lax.psum_scatter(jnp.einsum('tba,tan->tbn', gradient_token_tiles, retaine...]
    psum x2 -> x1, waiting for transfers between devices: 203 us -> 97.9 us  [body(): lax.psum(gram_of(moment).astype(BF16), 'expert').astype(jnp.float32)]
    all_gather x1 -> x0, waiting for transfers between devices: 88.9 us -> none  [body(): gathered = lax.all_gather(update_local[None], 'dp', axis=0, tiled=True)]
    all_gather x0 -> x1, blocking collectives: none -> 44.3 us  [body(): lax.all_gather(update_local.astype(jnp.float16)[None], 'dp', axis=0, tile...]
    dot_general x7 -> x8, matrix products: 90.1 us -> 53.8 us  [the longest x4 28.8 us: dot16(): jnp.dot(left.astype(BF16), right.astype(BF16), preferred_element_type=jnp...]
    all_to_all x0 -> x2, waiting for transfers between devices: none -> 20.5 us  [the longest x1 11.2 us: body(): lax.all_to_all(gradient_token_tiles, 'dp', 0, 2, tiled=True)[0]]
    all_to_all x0 -> x2, starting transfers between devices: none -> 7.75 us  [the longest x1 4.24 us: body(): lax.all_to_all(gradient_token_tiles, 'dp', 0, 2, tiled=True)[0]]
    convert_element_type x0 -> x1, other arithmetic: none -> 7.24 us  [body(): return (moment[None], gathered.astype(jnp.float32))]
  transfers between devices with their start and end apart: 4 -> 3, of which waited for: 4 -> 3; matrix products, arithmetic and copies ran while one was open for 2% -> 4% of each run, Pallas kernels for 0% -> 0%
where the time goes in v1:
time: 286 us; the launch traced here: 285 us
  waiting for transfers between devices  118 us (41%)
  matrix products  53.8 us (19%)
  blocking collectives  44.3 us (15%)
  local copies, waits for them, and re-layouts  34.8 us (12%)
  between operations  14.9 us (5%)
  other arithmetic  11.4 us (4%)
  starting transfers between devices  7.8 us (3%)
    psum x1, waiting for transfers between devices, body(): lax.psum(gram_of(moment).astype(BF16), 'expert').astype(jnp.float32)  97.9 us
    all_gather x1, blocking collectives, body(): lax.all_gather(update_local.astype(jnp.float16)[None], 'dp', axis=0, tile...  44.3 us
    unnamed x14, local copies, waits for them, and re-layouts  29.4 us
    dot_general x4, matrix products, dot16(): jnp.dot(left.astype(BF16), right.astype(BF16), preferred_element_type=jnp...  28.8 us
    all_to_all x1, waiting for transfers between devices, body(): lax.all_to_all(gradient_token_tiles, 'dp', 0, 2, tiled=True)[0]  11.2 us
    all_to_all x1, waiting for transfers between devices, body(): rows_all = lax.all_to_all(retained_entries, 'dp', 0, 1, tiled=True)[0]  9.36 us
    dot_general x1, matrix products, gram_of(): jnp.dot(high.T, high, preferred_element_type=jnp.float32) + cross + cross.T  9.3 us
    dot_general x1, matrix products, body(): jnp.dot(current, mixer, precision=lax.Precision.HIGH, preferred_element_t...  8.01 us
  transfers between devices with their start and end apart: 3, of which 3 were waited for; matrix products, arithmetic and copies ran while one was open for 4% of the time, Pallas kernels for 0%

profile of v1, /device:TPU:0, one launch (start us, length us, event | category | flops | bytes accessed | tf_op | source)
XLA Modules:
  0.0 285.4 jit_solution(13420966651316588153)
XLA Ops:
  7.2 0.0 copy-start.3
  7.2 2.3 copy.12
  9.5 4.2 %all-to-all-start.1 = ((bf16[4,896,128]{1,2,0:T(8,128)(2,1)}), bf16[4,896,128]{1,2,0:T(8,128)(2,1)S(1)}, u32[]{:S(2)}, u32[]{:S(2)}) async-start(bf16[4,896,128]{1,2,0:T(8,128)(2,1)} %copy.12), calls=%async_computation.1 | async-start | bytes 1835008 | tf_op jit(solution)/shard_map/all_to_all | solution.py:57
  13.7 0.7 multiply_bitcast_fusion
  14.4 0.1 iota_compare_fusion.1
  14.5 0.0 copy-done.3
  14.5 1.1 broadcast_select_fusion
  15.6 11.2 %all-to-all-done.1 = bf16[4,896,128]{1,2,0:T(8,128)(2,1)S(1)} async-done(((bf16[4,896,128]{1,2,0:T(8,128)(2,1)}), bf16[4,896,128]{1,2,0:T(8,128)(2,1)S(1)}, u32[]{:S(2)}, u32[]{:S(2)}) %all-to-all-start.1) | async-done | bytes 917536 | tf_op jit(solution)/shard_map/all_to_all | solution.py:57
  26.8 3.5 %all-to-all-start = ((bf16[4,128,1024]{2,1,0:T(8,128)(2,1)}), bf16[4,128,1024]{2,1,0:T(8,128)(2,1)S(1)}, u32[]{:S(2)}, u32[]{:S(2)}) async-start(bf16[4,128,1024]{2,1,0:T(8,128)(2,1)} %broadcast_select_fusion), calls=%async_computation | async-start | bytes 2097152 | tf_op jit(solution)/shard_map/all_to_all | solution.py:56
  30.3 0.0 all-reduce.2.cloned.1.call-start
  30.3 5.0 %copy.11 = f32[1,896,1024]{1,2,0:T(8,128)} copy(f32[1,896,1024]{2,1,0:T(8,128)} %param.6) | data formatting | bytes 7340032 | tf_op args[2]
  35.4 9.4 %all-to-all-done = bf16[4,128,1024]{2,1,0:T(8,128)(2,1)S(1)} async-done(((bf16[4,128,1024]{2,1,0:T(8,128)(2,1)}), bf16[4,128,1024]{2,1,0:T(8,128)(2,1)S(1)}, u32[]{:S(2)}, u32[]{:S(2)}) %all-to-all-start) | async-done | bytes 1048608 | tf_op jit(solution)/shard_map/all_to_all | solution.py:56
  44.7 3.3 %bitcast_add_fusion.1 = f32[896,1024]{0,1:T(8,128)S(1)} fusion(f32[1,896,1024]{1,2,0:T(8,128)} %copy.11, bf16[512,1024]{1,0:T(8,128)(2,1)S(1)} %bitcast.22, bf16[896,512]{0,1:T(8,128)(2,1)S(1)} %bitcast.23), kind=kOutput, calls=%fused_computation.17 | convolution fusion | flops 941359104 | bytes 9306112 | tf_op jit(solution)/shard_map/dot_general | solution.py:58
  48.1 0.0 copy-start
  48.1 1.8 copy-done
  49.9 4.4 %fusion.16 = f32[1024,1024]{1,0:T(8,128)} fusion(f32[896,1024]{0,1:T(8,128)S(1)} %bitcast_add_fusion.1), kind=kOutput, calls=%fused_computation.21 | convolution fusion | flops 1883635712 | bytes 7864320 | tf_op jit(solution)/shard_map/dot_general | solution.py:34
  54.2 5.4 %copy.13 = f32[1024,1024]{0,1:T(8,128)} copy(f32[1024,1024]{1,0:T(8,128)} %fusion.16) | data formatting | bytes 8388608 | tf_op jit(solution)/shard_map/dot_general | solution.py:34
  59.6 9.3 %fusion.6 = bf16[1024,1024]{1,0:T(8,128)(2,1)} fusion(f32[1024,1024]{0,1:T(8,128)} %copy.13, f32[1024,1024]{1,0:T(8,128)} %fusion.16, f32[896,1024]{0,1:T(8,128)} %copy-done), kind=kOutput, calls=%fused_computation.9 | convolution fusion | flops 1883111424 | bytes 14155776 | tf_op jit(solution)/shard_map/dot_general | solution.py:35
  68.9 0.0 all-reduce.2.cloned.1.call-update
  68.9 5.0 %copy.15 = f32[1,896,1024]{2,1,0:T(8,128)} copy(f32[1,896,1024]{1,2,0:T(8,128)} %bitcast.21) | data formatting | bytes 7340032
  73.9 97.9 %all-reduce.2.cloned.1.call-done = bf16[1024,1024]{1,0:T(8,128)(2,1)} async-done(((bf16[1024,1024]{1,0:T(8,128)(2,1)}), bf16[1024,1024]{1,0:T(8,128)(2,1)}) %all-reduce.2.cloned.1.call-update) | async-done | bytes 2097168 | tf_op jit(solution)/shard_map/psum | solution.py:60
  171.9 2.3 fusion.5
  174.9 0.0 copy-start.2
  174.9 7.5 %fusion.3 = f32[1024,1024]{1,0:T(8,128)} fusion(bf16[1024,1024]{1,0:T(8,128)(2,1)} %all-reduce.2.cloned.1.call-done, f32[]{:T(128)S(6)} %mul.85), kind=kOutput, calls=%fused_computation.5 | convolution fusion | flops 2155872256 | bytes 6291460 | tf_op jit(solution)/shard_map/dot_general | solution.py:24
  182.5 0.0 copy-done.2
  182.5 11.4 %fusion.22 = f32[1024,1024]{1,0:T(8,128)} fusion(f32[1024,1024]{1,0:T(8,128)} %fusion.3, bf16[1024,1024]{1,0:T(8,128)(2,1)S(1)} %copy-done.2, f32[]{:T(128)S(6)} %mul.85), kind=kOutput, calls=%fused_computation.26 | convolution fusion | flops 4302307328 | bytes 10485764 | tf_op jit(solution)/shard_map/dot_general | solution.py:24
  193.8 7.6 %multiply_add_fusion = f32[1024,1024]{1,0:T(8,128)S(1)} fusion(f32[1024,1024]{1,0:T(8,128)} %fusion.22, bf16[1024,1024]{1,0:T(8,128)(2,1)S(1)} %copy-done.2, f32[]{:T(128)S(6)} %mul.85), kind=kOutput, calls=%fused_computation.14 | convolution fusion | flops 2160066560 | bytes 10485764 | tf_op jit(solution)/shard_map/dot_general | solution.py:24
  201.4 2.3 fusion.23
  203.8 8.0 %multiply_convert_fusion = f16[896,1024]{0,1:T(8,128)(2,1)S(1)} fusion(f32[896,1024]{0,1:T(8,128)S(1)} %copy-done.1, f32[1024,1024]{1,0:T(8,128)S(1)} %fusion.23, f32[1024,1024]{1,0:T(8,128)S(1)} %copy-done.4, f32[1024,1024]{1,0:T(8,128)S(1)} %multiply_add_fusion, f32[]{:T(128)S(6)} %div.3), kind=kOutput, calls=%fused_computation.18 | convolution fusion | flops 5645795328 | bytes 18087940 | tf_op jit(solution)/shard_map/dot_general | solution.py:64
  211.8 44.3 %all-gather.2 = f16[3584,1024]{0,1:T(8,128)(2,1)S(1)} all-gather(f16[896,1024]{0,1:T(8,128)(2,1)S(1)} %multiply_convert_fusion), channel_id=2, replica_groups=mesh['dp'=4,'expert'=8] {'dp'}, dimensions={0}, use_global_device_ids=true | all-gather | bytes 9175040 | tf_op jit(solution)/shard_map/all_gather | solution.py:68
  256.0 7.2 %convert_element_type.53 = f32[3584,1024]{0,1:T(8,128)} convert(f16[3584,1024]{0,1:T(8,128)(2,1)S(1)} %all-gather.2) | non-fusion elementwise | flops 3670016 | bytes 22020096 | tf_op jit(solution)/shard_map/convert_element_type | solution.py:69
  263.3 15.3 %copy.18 = f32[3584,1024]{1,0:T(8,128)} copy(f32[3584,1024]{0,1:T(8,128)} %convert_element_type.53) | data formatting | bytes 29360128
  (4 shorter events, 0.0 us)
Async XLA Ops:
  7.2 7.3 %copy-start.3 = (bf16[4,128,1024]{2,1,0:T(8,128)(2,1)S(1)}, bf16[4,128,1024]{2,1,0:T(8,128)(2,1)}, u32[]{:S(2)}) copy-start(bf16[4,128,1024]{2,1,0:T(8,128)(2,1)} %param.4) | copy-start | bytes 3145732
  9.5 17.3 %all-to-all-start.1 = ((bf16[4,896,128]{1,2,0:T(8,128)(2,1)}), bf16[4,896,128]{1,2,0:T(8,128)(2,1)S(1)}, u32[]{:S(2)}, u32[]{:S(2)}) async-start(bf16[4,896,128]{1,2,0:T(8,128)(2,1)} %copy.12), calls=%async_computation.1 | async-start | bytes 1835008 | tf_op jit(solution)/shard_map/all_to_all | solution.py:57
  26.8 18.0 %all-to-all-start = ((bf16[4,128,1024]{2,1,0:T(8,128)(2,1)}), bf16[4,128,1024]{2,1,0:T(8,128)(2,1)S(1)}, u32[]{:S(2)}, u32[]{:S(2)}) async-start(bf16[4,128,1024]{2,1,0:T(8,128)(2,1)} %broadcast_select_fusion), calls=%async_computation | async-start | bytes 2097152 | tf_op jit(solution)/shard_map/all_to_all | solution.py:56
  30.3 141.6 %all-reduce.2.cloned.1.call-start = ((), (), s32[]{:S(2)}) async-start(), calls=%async_computation.2 | async-start | bytes 4194304 | tf_op jit(solution)/shard_map/psum | solution.py:60
  48.1 1.8 copy-start
  174.9 7.5 %copy-start.2 = (bf16[1024,1024]{1,0:T(8,128)(2,1)S(1)}, bf16[1024,1024]{1,0:T(8,128)(2,1)}, u32[]{:S(2)}) copy-start(bf16[1024,1024]{1,0:T(8,128)(2,1)} %all-reduce.2.cloned.1.call-done) | copy-start | bytes 6291460
  193.8 7.6 %copy-start.4 = (f32[1024,1024]{1,0:T(8,128)S(1)}, f32[1024,1024]{1,0:T(8,128)}, u32[]{:S(2)}) copy-start(f32[1024,1024]{1,0:T(8,128)} %fusion.3) | copy-start | bytes 12582916
  201.4 2.3 copy-start.1
Sparse Core Ops, SparseCore 0:
  69.1 102.7 all-reduce.1

commit v2 on v1

v2 whole, which is shorter than its diff:
```python
import functools
import math

import jax
import jax.numpy as jnp
from jax import lax
from jax.experimental import pallas as pl
from jax.experimental.pallas import tpu as pltpu
from jax.sharding import PartitionSpec as P

D = 7168
FF = 1024
TILE = 16
ITERS = 2


MOMENTUM_DECAY = 0.95
EPSILON = 1e-07
COEF_A = 3.4445
COEF_B = -4.775
COEF_C = 2.0315

BF16 = jnp.bfloat16
OUT = jnp.float32
MESH = pl.DeviceIdType.MESH


BLOCK = 256
PAIR = 2
CHUNKS = 5


def dot16(left, right):
    return jnp.dot(left, right, preferred_element_type=jnp.float32)


def across(left, right):
    return lax.dot_general(left, right, (((0,), (0,)), ((), ())), preferred_element_type=jnp.float32)


def iterate_kernel(
    n, scale, moment_ref, out_ref, high, low, work, near, part, far, done, full,
    gram, gram16, first, first16, second16, other, mix, mix_low,
    near_sem, far_sem, done_sem, full_sem,
):
    me = lax.axis_index("expert")
    half, place = lax.rem(me, PAIR), lax.div(me, PAIR)
    places = n // PAIR
    piece = BLOCK // places
    partner = me + 1 - 2 * half
    size = moment_ref.shape[1]
    blocks = size // BLOCK
    pairs = [(i, j) for i in range(blocks) for j in range(i, blocks)]

    def peer(offset):
        return lax.rem(place + offset, places)

    def device(at):
        return {"expert": at}

    barrier = pltpu.get_barrier_semaphore()
    pl.semaphore_signal(barrier, inc=1, device_id=device(partner), device_id_type=MESH)
    for offset in range(1, places):
        pl.semaphore_signal(
            barrier, inc=1, device_id=device(peer(offset) * PAIR + half), device_id_type=MESH
        )

    sends = []

    def send(source, target, sems, at, to):
        copy = pltpu.make_async_remote_copy(
            src_ref=source,
            dst_ref=target,
            send_sem=sems.at[(0, *at)],
            recv_sem=sems.at[(1, *at)],
            device_id=device(to),
            device_id_type=MESH,
        )
        copy.start()
        sends.append(copy)
        return copy

    near_copies, far_copies, done_copies, full_copies = {}, {}, {}, {}

    def send_near(chunk):
        near_copies[chunk] = send(
            work.at[chunk, 1 - half], near.at[chunk], near_sem, (chunk,), partner
        )

    def send_far(chunk):
        near_copies[chunk].wait_recv()
        total = work[chunk, half].astype(jnp.float32) + near[chunk].astype(jnp.float32)
        part[chunk] = total.astype(BF16)
        for offset in range(1, places):
            to = peer(offset)
            rows = pl.ds(pl.multiple_of(to * piece, piece), piece)
            far_copies[chunk, offset] = send(
                part.at[chunk, rows],
                far.at[chunk, offset],
                far_sem,
                (chunk, offset),
                to * PAIR + half,
            )

    def send_done(chunk):
        mine = pl.ds(pl.multiple_of(place * piece, piece), piece)
        total = part[chunk, mine].astype(jnp.float32)
        for offset in range(1, places):
            far_copies[chunk, offset].wait_recv()
            total = total + far[chunk, offset].astype(jnp.float32)
        done[chunk] = total.astype(BF16)
        full[chunk, half, mine] = total.astype(BF16)
        for offset in range(1, places):
            done_copies[chunk, offset] = send(
                done.at[chunk],
                full.at[chunk, half, mine],
                done_sem,
                (chunk, offset),
                peer(offset) * PAIR + half,
            )

    def wait_done(chunk):
        for offset in range(1, places):
            source = lax.rem(place + places - offset, places)
            rows = pl.ds(pl.multiple_of(source * piece, piece), piece)
            pltpu.make_async_remote_copy(
                src_ref=done.at[chunk],
                dst_ref=full.at[chunk, half, rows],
                send_sem=done_sem.at[0, chunk, offset],
                recv_sem=done_sem.at[1, chunk, offset],
                device_id=device(partner),
                device_id_type=MESH,
            ).wait_recv()

    def send_full(chunk):
        wait_done(chunk)
        full_copies[chunk] = send(
            full.at[chunk, half], full.at[chunk, half], full_sem, (chunk,), partner
        )

    moment = moment_ref[...]
    rounded = moment.astype(BF16)
    high[...] = rounded
    low[...] = (moment - rounded.astype(jnp.float32)).astype(BF16)
    at = 0
    for i in range(blocks):
        rows = slice(i * BLOCK, (i + 1) * BLOCK)
        rest = slice(i * BLOCK, size)
        strip = across(high[:, rows], high[:, rest])
        strip += across(high[:, rows], low[:, rest]) + across(low[:, rows], high[:, rest])
        for j in range(i, blocks):
            block = strip[:, (j - i) * BLOCK : (j - i + 1) * BLOCK]
            work[at // PAIR, at % PAIR] = block.astype(BF16)
            at += 1
        if i == 0:
            pl.semaphore_wait(barrier, places)
        for chunk in range(len(near_copies), at // PAIR):
            send_near(chunk)
    for step in range(CHUNKS + 2):
        if step < CHUNKS:
            send_far(step)
        if 0 <= step - 1 < CHUNKS:
            send_done(step - 1)
        if 0 <= step - 2:
            send_full(step - 2)
    for chunk in range(CHUNKS):
        pltpu.make_async_remote_copy(
            src_ref=full.at[chunk, half],
            dst_ref=full.at[chunk, 1 - half],
            send_sem=full_sem.at[0, chunk],
            recv_sem=full_sem.at[1, chunk],
            device_id=device(partner),
            device_id_type=MESH,
        ).wait_recv()
    for copy in sends:
        copy.wait_send()

    trace = jnp.zeros((1, 1), jnp.float32)
    row_at = lax.broadcasted_iota(jnp.int32, (BLOCK, BLOCK), 0)
    col_at = lax.broadcasted_iota(jnp.int32, (BLOCK, BLOCK), 1)
    for at, (i, j) in enumerate(pairs):
        block = full[at // PAIR, at % PAIR].astype(jnp.float32)
        if i == j:
            trace += jnp.sum(jnp.where(row_at == col_at, block, 0.0), keepdims=True)
        gram[i * BLOCK : (i + 1) * BLOCK, j * BLOCK : (j + 1) * BLOCK] = block
        if i != j:
            gram[j * BLOCK : (j + 1) * BLOCK, i * BLOCK : (i + 1) * BLOCK] = block.T
    factor = 1.0 / (jnp.sqrt(trace) + EPSILON)

    def strips(step):
        @pl.loop(0, blocks)
        def _(i):
            step(pl.ds(pl.multiple_of(i * BLOCK, BLOCK), BLOCK))

    def scaled(rows):
        value = gram[rows] * (factor * factor)
        gram[rows] = value
        gram16[rows] = value.astype(BF16)

    def mix_first(rows):
        value = COEF_B * gram[rows] + COEF_C * dot16(gram16[rows], gram16[...])
        first[rows] = value
        first16[rows] = value.astype(BF16)

    def mix_square(rows):
        value = 2.0 * COEF_A * first[rows] + dot16(first16[rows], first16[...])
        other[rows] = value.astype(BF16)

    def next_gram(rows):
        value = COEF_A * COEF_A * gram[rows] + dot16(gram16[rows], other[...])
        gram[rows] = value
        mix[rows] = value.astype(BF16)

    def mix_second(rows):
        value = COEF_B * gram[rows] + COEF_C * dot16(mix[rows], mix[...])
        gram[rows] = value
        second16[rows] = value.astype(BF16)

    def mix_both(rows):
        value = COEF_A * (first[rows] + gram[rows]) + dot16(first16[rows], second16[...])
        top = value.astype(BF16)
        gram16[rows] = top
        mix_low[rows] = (value - top.astype(jnp.float32)).astype(BF16)

    for step in (scaled, mix_first, mix_square, next_gram, mix_second, mix_both):
        strips(step)

    tall = moment_ref.shape[0]
    stride = math.gcd(tall, 128)

    @pl.loop(0, tall // stride)
    def _(i):
        rows = pl.ds(pl.multiple_of(i * stride, stride), stride)
        value = dot16(high[rows], gram16[...]) + dot16(low[rows], gram16[...])
        value += dot16(high[rows], mix_low[...]) + COEF_A * COEF_A * moment_ref[rows]
        out_ref[rows] = (value * (factor * scale)).astype(out_ref.dtype)


def iterated(moment, n):
    tall, size = moment.shape
    square = (size, size)
    places = n // PAIR
    piece = BLOCK // places
    vmem, dma = pltpu.VMEM, pltpu.SemaphoreType.DMA
    scratch = [vmem((tall, size), BF16)] * 2 + [
        vmem((CHUNKS, PAIR, BLOCK, BLOCK), BF16),
        vmem((CHUNKS, BLOCK, BLOCK), BF16),
        vmem((CHUNKS, BLOCK, BLOCK), BF16),
        vmem((CHUNKS, places, piece, BLOCK), BF16),
        vmem((CHUNKS, piece, BLOCK), BF16),
        vmem((CHUNKS, PAIR, BLOCK, BLOCK), BF16),
        vmem(square, jnp.float32),
        vmem(square, BF16),
        vmem(square, jnp.float32),
        vmem(square, BF16),
        vmem(square, BF16),
        vmem(square, BF16),
        vmem(square, BF16),
        vmem(square, BF16),
        dma((2, CHUNKS)),
        dma((2, CHUNKS, places)),
        dma((2, CHUNKS, places)),
        dma((2, CHUNKS)),
    ]
    return pl.pallas_call(
        functools.partial(iterate_kernel, n, math.sqrt(max(FF, D))),
        out_shape=jax.ShapeDtypeStruct(moment.shape, OUT),
        in_specs=[pl.BlockSpec(memory_space=pltpu.VMEM)],
        out_specs=pl.BlockSpec(memory_space=pltpu.VMEM),
        scratch_shapes=scratch,
        compiler_params=pltpu.CompilerParams(
            collective_id=0, has_side_effects=True, vmem_limit_bytes=56 * 2**20
        ),
    )(moment)


def body(hidden_token_tiles, gradient_token_tiles, momentum, filled_tile_count):
    group = lax.axis_index("dp")
    rows_group = hidden_token_tiles.shape[1]
    experts_here = hidden_token_tiles.shape[0]
    limits = lax.dynamic_index_in_dim(filled_tile_count, group, 0, keepdims=False) * TILE
    positions = lax.broadcasted_iota(jnp.int32, (experts_here, rows_group), 1)
    tallied_tiles = positions < limits[:, None]
    retained_entries = jnp.where(
        tallied_tiles[:, :, None], hidden_token_tiles, jnp.zeros((), jnp.bfloat16)
    )
    rows_all = lax.all_to_all(retained_entries, "dp", 0, 1, tiled=True)[0]
    columns_all = lax.all_to_all(gradient_token_tiles, "dp", 0, 2, tiled=True)[0]
    gradient = jnp.dot(columns_all, rows_all, preferred_element_type=jnp.float32)
    moment = MOMENTUM_DECAY * momentum[0] + gradient
    update_local = iterated(moment, lax.axis_size("expert"))
    gathered = lax.all_gather(update_local.astype(jnp.float16)[None], "dp", axis=0, tiled=True)
    return (moment[None], gathered.astype(jnp.float32))


def solution(mesh):
    placed = (P(None, "dp", None), P(None, "expert", "dp"), P("dp", "expert", None), P())
    return jax.shard_map(
        body,
        mesh=mesh,
        in_specs=placed,
        out_specs=(P("dp", "expert", None), P(None, "expert", None)),
        check_vma=False,
    )
```

time: 286 us -> 168 us (0.59)
  waiting for transfers between devices: 118 us -> 12.1 us
  Pallas kernels: 0 us -> 71.5 us
  matrix products: 53.8 us -> 5.06 us
  local copies, waits for them, and re-layouts: 34.8 us -> 2.31 us
  blocking collectives: 44.3 us -> 60.5 us
  between operations: 14.9 us -> 0.67 us
  starting transfers between devices: 7.8 us -> 4.24 us
    psum x1 -> x0, waiting for transfers between devices: 97.9 us -> none  [body(): lax.psum(gram_of(moment).astype(BF16), 'expert').astype(jnp.float32)]
    pallas_call x0 -> x1, Pallas kernels: none -> 71.5 us  [iterated(): pl.pallas_call(functools.partial(iterate_kernel, n, math.sqrt(max(FF, D))...]
    dot_general x7 -> x0, matrix products: 50.5 us -> none  [the longest x4 28.8 us: dot16(): jnp.dot(left.astype(BF16), right.astype(BF16), preferred_element_type=jnp...]
    unnamed x14 -> x3, local copies, waits for them, and re-layouts: 29.4 us -> 2.31 us
    all_to_all x0 -> x1, blocking collectives: none -> 16.9 us  [body(): rows_all = lax.all_to_all(retained_entries, 'dp', 0, 1, tiled=True)[0]]
    all_to_all x1 -> x0, waiting for transfers between devices: 9.36 us -> none  [body(): rows_all = lax.all_to_all(retained_entries, 'dp', 0, 1, tiled=True)[0]]
    dot_general x1 -> x0, local copies, waits for them, and re-layouts: 5.36 us -> none  [gram_of(): cross = jnp.dot(high.T, low, preferred_element_type=jnp.float32)]
    all_to_all x1 -> x0, starting transfers between devices: 3.52 us -> none  [body(): rows_all = lax.all_to_all(retained_entries, 'dp', 0, 1, tiled=True)[0]]
  transfers between devices with their start and end apart: 3 -> 1, of which waited for: 3 -> 1; matrix products, arithmetic and copies ran while one was open for 4% -> 1% of each run, Pallas kernels for 0% -> 0%
where the time goes in v2:
time: 168 us; the launch traced here: 167 us
  Pallas kernels  71.5 us (43%)
  blocking collectives  60.5 us (36%)
  waiting for transfers between devices  12.1 us (7%)
  other arithmetic  10.8 us (6%)
  matrix products  5.06 us (3%)
  starting transfers between devices  4.24 us (3%)
  local copies, waits for them, and re-layouts  2.31 us (1%)
    pallas_call x1, Pallas kernels, iterated(): pl.pallas_call(functools.partial(iterate_kernel, n, math.sqrt(max(FF, D))...  71.5 us
    all_gather x1, blocking collectives, body(): lax.all_gather(update_local.astype(jnp.float16)[None], 'dp', axis=0, tile...  43.6 us
    all_to_all x1, blocking collectives, body(): rows_all = lax.all_to_all(retained_entries, 'dp', 0, 1, tiled=True)[0]  16.9 us
    all_to_all x1, waiting for transfers between devices, body(): lax.all_to_all(gradient_token_tiles, 'dp', 0, 2, tiled=True)[0]  12.1 us
    convert_element_type x1, other arithmetic, body(): return (moment[None], gathered.astype(jnp.float32))  7.49 us
    dot_general x1, matrix products, body(): jnp.dot(columns_all, rows_all, preferred_element_type=jnp.float32)  5.06 us
    all_to_all x1, starting transfers between devices, body(): lax.all_to_all(gradient_token_tiles, 'dp', 0, 2, tiled=True)[0]  4.24 us
  transfers between devices with their start and end apart: 1, of which 1 were waited for; matrix products, arithmetic and copies ran while one was open for 1% of the time, Pallas kernels for 0%

profile of v2, /device:TPU:0, one launch (start us, length us, event | category | flops | bytes accessed | tf_op | source)
XLA Modules:
  0.0 167.1 jit_solution(10761150044214318201)
XLA Ops:
  0.6 0.0 copy-start
  0.6 2.3 %copy.7 = bf16[4,896,128]{1,2,0:T(8,128)(2,1)} copy(bf16[4,896,128]{2,1,0:T(8,128)(2,1)} %param.5) | data formatting | bytes 1835008 | tf_op args[1]
  2.9 4.2 %all-to-all-start.1 = ((bf16[4,896,128]{1,2,0:T(8,128)(2,1)}), bf16[4,896,128]{1,2,0:T(8,128)(2,1)S(1)}, u32[]{:S(2)}, u32[]{:S(2)}) async-start(bf16[4,896,128]{1,2,0:T(8,128)(2,1)} %copy.7), calls=%async_computation.1 | async-start | bytes 1835008 | tf_op jit(solution)/shard_map/all_to_all | solution.py:288
  7.2 0.7 multiply_bitcast_fusion
  7.9 0.1 iota_compare_fusion
  7.9 0.0 copy-done
  7.9 0.1 broadcast_select_fusion
  8.1 12.1 %all-to-all-done.1 = bf16[4,896,128]{1,2,0:T(8,128)(2,1)S(1)} async-done(((bf16[4,896,128]{1,2,0:T(8,128)(2,1)}), bf16[4,896,128]{1,2,0:T(8,128)(2,1)S(1)}, u32[]{:S(2)}, u32[]{:S(2)}) %all-to-all-start.1) | async-done | bytes 917536 | tf_op jit(solution)/shard_map/all_to_all | solution.py:288
  20.2 16.9 %all_to_all.24 = bf16[4,128,1024]{2,1,0:T(8,128)(2,1)S(1)} all-to-all(bf16[4,128,1024]{2,1,0:T(8,128)(2,1)S(1)} %broadcast_select_fusion), channel_id=1, replica_groups=mesh['dp'=4,'expert'=8] {'dp'}, dimensions={0} | all-to-all | bytes 2097152 | tf_op jit(solution)/shard_map/all_to_all | solution.py:287
  37.1 5.1 %bitcast_add_fusion.moment_ref = f32[896,1024]{1,0:T(8,128)} fusion(f32[1,896,1024]{2,1,0:T(8,128)} %param.6, bf16[512,1024]{1,0:T(8,128)(2,1)S(1)} %bitcast.19, bf16[896,512]{0,1:T(8,128)(2,1)S(1)} %bitcast.20), kind=kOutput, calls=%fused_computation | convolution fusion | flops 941359104 | bytes 9306112 | tf_op jit(solution)/shard_map/dot_general | solution.py:289
  42.2 71.5 %shard_map.59 = f32[896,1024]{1,0:T(8,128)} custom-call(f32[896,1024]{1,0:T(8,128)} %bitcast_add_fusion.moment_ref), custom_call_target="tpu_custom_call" | custom-call | tf_op jit(solution)/shard_map/pallas_call | solution.py:265
  113.7 2.4 %convert_element_type.6 = f16[896,1024]{1,0:T(8,128)(2,1)S(1)} convert(f32[896,1024]{1,0:T(8,128)} %shard_map.59) | non-fusion elementwise | flops 917504 | bytes 5505024 | tf_op jit(solution)/shard_map/convert_element_type | solution.py:292
  116.1 43.6 %all-gather.2 = f16[3584,1024]{1,0:T(8,128)(2,1)S(1)} all-gather(f16[896,1024]{1,0:T(8,128)(2,1)S(1)} %convert_element_type.6), channel_id=2, replica_groups=mesh['dp'=4,'expert'=8] {'dp'}, dimensions={0}, use_global_device_ids=true | all-gather | bytes 9175040 | tf_op jit(solution)/shard_map/all_gather | solution.py:292
  159.7 7.5 %convert = f32[4,896,1024]{2,1,0:T(8,128)} convert(f16[4,896,1024]{2,1,0:T(8,128)(2,1)S(1)} %bitcast.17) | non-fusion elementwise | flops 3670016 | bytes 22020096 | tf_op jit(solution)/shard_map/convert_element_type | solution.py:293
Async XLA Ops:
  0.6 7.3 %copy-start = (bf16[4,128,1024]{2,1,0:T(8,128)(2,1)S(1)}, bf16[4,128,1024]{2,1,0:T(8,128)(2,1)}, u32[]{:S(2)}) copy-start(bf16[4,128,1024]{2,1,0:T(8,128)(2,1)} %param.4) | copy-start | bytes 3145732
  2.9 17.3 %all-to-all-start.1 = ((bf16[4,896,128]{1,2,0:T(8,128)(2,1)}), bf16[4,896,128]{1,2,0:T(8,128)(2,1)S(1)}, u32[]{:S(2)}, u32[]{:S(2)}) async-start(bf16[4,896,128]{1,2,0:T(8,128)(2,1)} %copy.7), calls=%async_computation.1 | async-start | bytes 1835008 | tf_op jit(solution)/shard_map/all_to_all | solution.py:288

commit v3 on v2

--- a/solution.py
+++ b/solution.py
@@ -21,7 +21,7 @@
 COEF_C = 2.0315
 
 BF16 = jnp.bfloat16
-OUT = jnp.float32
+LEVELS = 32700.0
 MESH = pl.DeviceIdType.MESH
 
 
@@ -39,11 +39,13 @@
 
 
 def iterate_kernel(
-    n, scale, moment_ref, out_ref, high, low, work, near, part, far, done, full,
-    gram, gram16, first, first16, second16, other, mix, mix_low,
-    near_sem, far_sem, done_sem, full_sem,
+    n, groups, scale, moment_ref, code_ref, top_ref, high, low, work, near, part, far, done, full,
+    gram, gram16, first, first16, second16, other, mix, mix_low, code, top,
+    near_sem, far_sem, done_sem, full_sem, twin_sem, group_sem, pass_sem, top_sem, local_sem,
 ):
     me = lax.axis_index("expert")
+    group = lax.axis_index("dp")
+    twin = group + 1 - 2 * lax.rem(group, PAIR)
     half, place = lax.rem(me, PAIR), lax.div(me, PAIR)
     places = n // PAIR
     piece = BLOCK // places
@@ -65,6 +67,14 @@
             barrier, inc=1, device_id=device(peer(offset) * PAIR + half), device_id_type=MESH
         )
 
+    for offset in range(1, groups):
+        pl.semaphore_signal(
+            barrier,
+            inc=1,
+            device_id={"dp": lax.rem(group + offset, groups)},
+            device_id_type=MESH,
+        )
+
     sends = []
 
     def send(source, target, sems, at, to):
@@ -73,7 +83,7 @@
             dst_ref=target,
             send_sem=sems.at[(0, *at)],
             recv_sem=sems.at[(1, *at)],
-            device_id=device(to),
+            device_id=to if isinstance(to, dict) else device(to),
             device_id_type=MESH,
         )
         copy.start()
@@ -153,7 +163,7 @@
             work[at // PAIR, at % PAIR] = block.astype(BF16)
             at += 1
         if i == 0:
-            pl.semaphore_wait(barrier, places)
+            pl.semaphore_wait(barrier, places + groups - 1)
         for chunk in range(len(near_copies), at // PAIR):
             send_near(chunk)
     for step in range(CHUNKS + 2):
@@ -172,9 +182,6 @@
             device_id=device(partner),
             device_id_type=MESH,
         ).wait_recv()
-    for copy in sends:
-        copy.wait_send()
-
     trace = jnp.zeros((1, 1), jnp.float32)
     row_at = lax.broadcasted_iota(jnp.int32, (BLOCK, BLOCK), 0)
     col_at = lax.broadcasted_iota(jnp.int32, (BLOCK, BLOCK), 1)
@@ -225,22 +232,73 @@
     for step in (scaled, mix_first, mix_square, next_gram, mix_second, mix_both):
         strips(step)
 
-    tall = moment_ref.shape[0]
-    stride = math.gcd(tall, 128)
-
-    @pl.loop(0, tall // stride)
-    def _(i):
-        rows = pl.ds(pl.multiple_of(i * stride, stride), stride)
+    stride = code.shape[1]
+    parts = code.shape[0]
+    locals_ = []
+    group_copies = {}
+    top[...] = jnp.zeros_like(top)
+    for i in range(parts):
+        rows = slice(i * stride, (i + 1) * stride)
         value = dot16(high[rows], gram16[...]) + dot16(low[rows], gram16[...])
         value += dot16(high[rows], mix_low[...]) + COEF_A * COEF_A * moment_ref[rows]
-        out_ref[rows] = (value * (factor * scale)).astype(out_ref.dtype)
-
-
-def iterated(moment, n):
+        value = value * (factor * scale)
+        peak = jnp.maximum(jnp.max(jnp.abs(value), axis=0, keepdims=True), 1e-30)
+        top[i : i + 1] = peak * (1.0 / LEVELS)
+        code[i] = jnp.round(value * (LEVELS / peak)).astype(jnp.int32).astype(jnp.int16)
+        place_here = code_ref.at[group, i]
+        for offset in range(1, groups // PAIR):
+            to = {"dp": lax.rem(group + PAIR * offset, groups)}
+            group_copies[i, offset] = send(code.at[i], place_here, group_sem, (i, offset), to)
+        send(code.at[i], place_here, twin_sem, (i,), {"dp": twin})
+        copy = pltpu.make_async_copy(code.at[i], place_here, local_sem.at[i])
+        copy.start()
+        locals_.append(copy)
+    for offset in range(1, groups):
+        to = {"dp": lax.rem(group + offset, groups)}
+        send(top, top_ref.at[group], top_sem, (offset,), to)
+    copy = pltpu.make_async_copy(top, top_ref.at[group], local_sem.at[parts])
+    copy.start()
+    locals_.append(copy)
+
+    def arrival(target, sems, at):
+        pltpu.make_async_remote_copy(
+            src_ref=target,
+            dst_ref=target,
+            send_sem=sems.at[(0, *at)],
+            recv_sem=sems.at[(1, *at)],
+            device_id={"dp": twin},
+            device_id_type=MESH,
+        ).wait_recv()
+
+    for i in range(parts):
+        for offset in range(1, groups // PAIR):
+            source = lax.rem(group + groups - PAIR * offset, groups)
+            there = code_ref.at[source, i]
+            arrival(there, group_sem, (i, offset))
+            send(there, there, pass_sem, (i, offset), {"dp": twin})
+    for i in range(parts):
+        arrival(code_ref.at[twin, i], twin_sem, (i,))
+        for offset in range(1, groups // PAIR):
+            source = lax.rem(twin + groups - PAIR * offset, groups)
+            arrival(code_ref.at[source, i], pass_sem, (i, offset))
+    for offset in range(1, groups):
+        source = lax.rem(group + groups - offset, groups)
+        arrival(top_ref.at[source], top_sem, (offset,))
+    for copy in sends:
+        copy.wait_send()
+    for copy in locals_:
+        copy.wait()
+
+
+def iterated(moment, n, groups):
     tall, size = moment.shape
     square = (size, size)
     places = n // PAIR
     piece = BLOCK // places
+    stride = math.gcd(tall, 128)
+    parts = tall // stride
+    tops = -(-parts // 8) * 8
+    links = groups // PAIR
     vmem, dma = pltpu.VMEM, pltpu.SemaphoreType.DMA
     scratch = [vmem((tall, size), BF16)] * 2 + [
         vmem((CHUNKS, PAIR, BLOCK, BLOCK), BF16),
@@ -257,21 +315,33 @@
         vmem(square, BF16),
         vmem(square, BF16),
         vmem(square, BF16),
+        vmem((parts, stride, size), jnp.int16),
+        vmem((tops, size), jnp.float32),
         dma((2, CHUNKS)),
         dma((2, CHUNKS, places)),
         dma((2, CHUNKS, places)),
         dma((2, CHUNKS)),
+        dma((2, parts)),
+        dma((2, parts, links)),
+        dma((2, parts, links)),
+        dma((2, groups)),
+        dma((parts + 1,)),
     ]
-    return pl.pallas_call(
-        functools.partial(iterate_kernel, n, math.sqrt(max(FF, D))),
-        out_shape=jax.ShapeDtypeStruct(moment.shape, OUT),
+    code, top = pl.pallas_call(
+        functools.partial(iterate_kernel, n, groups, math.sqrt(max(FF, D))),
+        out_shape=(
+            jax.ShapeDtypeStruct((groups, parts, stride, size), jnp.int16),
+            jax.ShapeDtypeStruct((groups, tops, size), jnp.float32),
+        ),
         in_specs=[pl.BlockSpec(memory_space=pltpu.VMEM)],
-        out_specs=pl.BlockSpec(memory_space=pltpu.VMEM),
+        out_specs=(pl.BlockSpec(memory_space=pl.ANY),) * 2,
         scratch_shapes=scratch,
         compiler_params=pltpu.CompilerParams(
             collective_id=0, has_side_effects=True, vmem_limit_bytes=56 * 2**20
         ),
     )(moment)
+    update = code.astype(jnp.float32) * top[:, :parts, None]
+    return update.reshape(groups, tall, size)
 
 
 def body(hidden_token_tiles, gradient_token_tiles, momentum, filled_tile_count):
@@ -288,9 +358,8 @@
     columns_all = lax.all_to_all(gradient_token_tiles, "dp", 0, 2, tiled=True)[0]
     gradient = jnp.dot(columns_all, rows_all, preferred_element_type=jnp.float32)
     moment = MOMENTUM_DECAY * momentum[0] + gradient
-    update_local = iterated(moment, lax.axis_size("expert"))
-    gathered = lax.all_gather(update_local.astype(jnp.float16)[None], "dp", axis=0, tiled=True)
-    return (moment[None], gathered.astype(jnp.float32))
+    update = iterated(moment, lax.axis_size("expert"), lax.axis_size("dp"))
+    return (moment[None], update)
 
 
 def solution(mesh):

time: 168 us -> 159 us (0.946)
  blocking collectives: 60.5 us -> 16.9 us
  Pallas kernels: 71.5 us -> 105 us
    all_gather x1 -> x0, blocking collectives: 43.6 us -> none  [body(): lax.all_gather(update_local.astype(jnp.float16)[None], 'dp', axis=0, tile...]
    pallas_call x1, Pallas kernels: 71.5 us -> 105 us  [iterated(): pl.pallas_call(functools.partial(iterate_kernel, n, groups, math.sqrt(max...]
    mul x0 -> x1, other arithmetic: none -> 11.2 us  [iterated(): update = code.astype(jnp.float32) * top[:, :parts, None]]
    convert_element_type x2 -> x0, other arithmetic: 9.88 us -> none  [the longest x1 7.49 us: body(): return (moment[None], gathered.astype(jnp.float32))]
where the time goes in v3:
time: 159 us; the launch traced here: 158 us
  Pallas kernels  105 us (66%)
  blocking collectives  16.9 us (11%)
  other arithmetic  12.1 us (8%)
  waiting for transfers between devices  12.1 us (8%)
  matrix products  5.06 us (3%)
  starting transfers between devices  4.24 us (3%)
  local copies, waits for them, and re-layouts  2.31 us (1%)
    pallas_call x1, Pallas kernels, iterated(): pl.pallas_call(functools.partial(iterate_kernel, n, groups, math.sqrt(max...  105 us
    all_to_all x1, blocking collectives, body(): rows_all = lax.all_to_all(retained_entries, 'dp', 0, 1, tiled=True)[0]  16.9 us
    all_to_all x1, waiting for transfers between devices, body(): lax.all_to_all(gradient_token_tiles, 'dp', 0, 2, tiled=True)[0]  12.1 us
    mul x1, other arithmetic, iterated(): update = code.astype(jnp.float32) * top[:, :parts, None]  11.2 us
    dot_general x1, matrix products, body(): jnp.dot(columns_all, rows_all, preferred_element_type=jnp.float32)  5.06 us
    all_to_all x1, starting transfers between devices, body(): lax.all_to_all(gradient_token_tiles, 'dp', 0, 2, tiled=True)[0]  4.24 us
  transfers between devices with their start and end apart: 1, of which 1 were waited for; matrix products, arithmetic and copies ran while one was open for 1% of the time, Pallas kernels for 0%

profile of v3, /device:TPU:0, one launch (start us, length us, event | category | flops | bytes accessed | tf_op | source)
XLA Modules:
  0.0 158.5 jit_solution(16928591535157553970)
XLA Ops:
  0.6 0.0 copy-start
  0.6 2.3 %copy.7 = bf16[4,896,128]{1,2,0:T(8,128)(2,1)} copy(bf16[4,896,128]{2,1,0:T(8,128)(2,1)} %param.5) | data formatting | bytes 1835008 | tf_op args[1]
  2.9 4.2 %all-to-all-start.1 = ((bf16[4,896,128]{1,2,0:T(8,128)(2,1)}), bf16[4,896,128]{1,2,0:T(8,128)(2,1)S(1)}, u32[]{:S(2)}, u32[]{:S(2)}) async-start(bf16[4,896,128]{1,2,0:T(8,128)(2,1)} %copy.7), calls=%async_computation.1 | async-start | bytes 1835008 | tf_op jit(solution)/shard_map/all_to_all | solution.py:358
  7.2 0.7 multiply_bitcast_fusion
  7.9 0.1 iota_compare_fusion
  7.9 0.0 copy-done
  7.9 0.1 broadcast_select_fusion
  8.1 12.1 %all-to-all-done.1 = bf16[4,896,128]{1,2,0:T(8,128)(2,1)S(1)} async-done(((bf16[4,896,128]{1,2,0:T(8,128)(2,1)}), bf16[4,896,128]{1,2,0:T(8,128)(2,1)S(1)}, u32[]{:S(2)}, u32[]{:S(2)}) %all-to-all-start.1) | async-done | bytes 917536 | tf_op jit(solution)/shard_map/all_to_all | solution.py:358
  20.2 16.9 %all_to_all.24 = bf16[4,128,1024]{2,1,0:T(8,128)(2,1)S(1)} all-to-all(bf16[4,128,1024]{2,1,0:T(8,128)(2,1)S(1)} %broadcast_select_fusion), channel_id=1, replica_groups=mesh['dp'=4,'expert'=8] {'dp'}, dimensions={0} | all-to-all | bytes 2097152 | tf_op jit(solution)/shard_map/all_to_all | solution.py:357
  37.1 5.1 %bitcast_add_fusion.moment_ref = f32[896,1024]{1,0:T(8,128)} fusion(f32[1,896,1024]{2,1,0:T(8,128)} %param.6, bf16[512,1024]{1,0:T(8,128)(2,1)S(1)} %bitcast.19, bf16[896,512]{0,1:T(8,128)(2,1)S(1)} %bitcast.20), kind=kOutput, calls=%fused_computation.1 | convolution fusion | flops 941359104 | bytes 9306112 | tf_op jit(solution)/shard_map/dot_general | solution.py:359
  42.2 105.1 %shard_map.59 = (s16[4,7,128,1024]{3,2,1,0:T(8,128)(2,1)}, f32[4,8,1024]{2,1,0:T(8,128)}) custom-call(f32[896,1024]{1,0:T(8,128)} %bitcast_add_fusion.moment_ref), custom_call_target="tpu_custom_call" | custom-call | tf_op jit(solution)/shard_map/pallas_call | solution.py:330
  147.3 11.2 %convert_multiply_fusion = f32[4,7,128,1024]{3,2,1,0:T(8,128)} fusion(s16[4,7,128,1024]{3,2,1,0:T(8,128)(2,1)} %get-tuple-element.4, f32[4,7,1024]{2,1,0:T(8,128)} %bitcast.21), kind=kLoop, calls=%fused_computation | loop fusion | flops 7340032 | bytes 22134784 | tf_op jit(solution)/shard_map/mul | solution.py:343
Async XLA Ops:
  0.6 7.3 %copy-start = (bf16[4,128,1024]{2,1,0:T(8,128)(2,1)S(1)}, bf16[4,128,1024]{2,1,0:T(8,128)(2,1)}, u32[]{:S(2)}) copy-start(bf16[4,128,1024]{2,1,0:T(8,128)(2,1)} %param.4) | copy-start | bytes 3145732
  2.9 17.3 %all-to-all-start.1 = ((bf16[4,896,128]{1,2,0:T(8,128)(2,1)}), bf16[4,896,128]{1,2,0:T(8,128)(2,1)S(1)}, u32[]{:S(2)}, u32[]{:S(2)}) async-start(bf16[4,896,128]{1,2,0:T(8,128)(2,1)} %copy.7), calls=%async_computation.1 | async-start | bytes 1835008 | tf_op jit(solution)/shard_map/all_to_all | solution.py:358

commit v4 on v3

--- a/solution.py
+++ b/solution.py
@@ -27,6 +27,7 @@
 
 BLOCK = 256
 PAIR = 2
+TEAM = 4
 CHUNKS = 5
 
 
@@ -36,6 +37,177 @@
 
 def across(left, right):
     return lax.dot_general(left, right, (((0,), (0,)), ((), ())), preferred_element_type=jnp.float32)
+
+
+def exchange_kernel(
+    n, groups, tiles_ref, hidden_ref, columns_ref, rows_ref,
+    twin_sem, tile_sem, piece_sem, pass_sem, local_sem,
+):
+    me = lax.axis_index("expert")
+    group = lax.axis_index("dp")
+    twin = group + 1 - 2 * lax.rem(group, PAIR)
+    member = lax.rem(me, TEAM)
+    team = me - member
+    deep = hidden_ref.shape[1]
+    piece = deep // TEAM
+    hops = range(1, groups // PAIR)
+
+    barrier = pltpu.get_barrier_semaphore()
+    for offset in range(1, groups):
+        to = {"dp": lax.rem(group + offset, groups)}
+        pl.semaphore_signal(barrier, inc=1, device_id=to, device_id_type=MESH)
+    for offset in range(1, TEAM):
+        to = {"expert": team + lax.rem(member + offset, TEAM)}
+        pl.semaphore_signal(barrier, inc=1, device_id=to, device_id_type=MESH)
+
+    def slot(at):
+        return columns_ref.at[:, pl.ds(pl.multiple_of(at * deep, deep), deep)]
+
+    def strip(ref, at, which):
+        return ref.at[at, pl.ds(pl.multiple_of(which * piece, piece), piece)]
+
+    local = [
+        pltpu.make_async_copy(hidden_ref.at[group], rows_ref.at[group], local_sem.at[0]),
+        pltpu.make_async_copy(tiles_ref.at[group], slot(group), local_sem.at[1]),
+    ]
+    for copy in local:
+        copy.start()
+    pl.semaphore_wait(barrier, groups - 1 + TEAM - 1)
+
+    def copy_of(source, target, sems, at, to):
+        return pltpu.make_async_remote_copy(
+            src_ref=source,
+            dst_ref=target,
+            send_sem=sems.at[(0, *at)],
+            recv_sem=sems.at[(1, *at)],
+            device_id=to,
+            device_id_type=MESH,
+        )
+
+    sends, arrivals = [], []
+
+    def send(*copy):
+        sends.append(copy_of(*copy))
+        sends[-1].start()
+
+    def arrival(target, sems, at):
+        return copy_of(target, target, sems, at, {"dp": twin})
+
+    for hop in hops:
+        for kind, base in enumerate((group, twin)):
+            to = lax.rem(base + PAIR * hop, groups)
+            send(
+                strip(hidden_ref, to, member), strip(rows_ref, group, member),
+                piece_sem, (kind, hop), {"dp": to},
+            )
+    for hop in hops:
+        for kind, base in enumerate((group, twin)):
+            to = lax.rem(base + PAIR * hop, groups)
+            send(tiles_ref.at[to], slot(group), tile_sem, (kind, hop), {"dp": to})
+    send(hidden_ref.at[twin], rows_ref.at[group], twin_sem, (0,), {"dp": twin})
+    send(tiles_ref.at[twin], slot(group), twin_sem, (1,), {"dp": twin})
+    for hop in hops:
+        for kind, base in enumerate((group, twin)):
+            source = lax.rem(base + groups - PAIR * hop, groups)
+            mine = strip(rows_ref, source, member)
+            arrival(mine, piece_sem, (kind, hop)).wait_recv()
+            for offset in range(1, TEAM):
+                to = {"expert": team + lax.rem(member + offset, TEAM)}
+                send(mine, mine, pass_sem, (kind, hop, offset), to)
+                other = lax.rem(member + TEAM - offset, TEAM)
+                arrivals.append(
+                    arrival(strip(rows_ref, source, other), pass_sem, (kind, hop, offset))
+                )
+            arrivals.append(arrival(slot(source), tile_sem, (kind, hop)))
+    arrivals.append(arrival(rows_ref.at[twin], twin_sem, (0,)))
+    arrivals.append(arrival(slot(twin), twin_sem, (1,)))
+    for copy in arrivals:
+        copy.wait_recv()
+    for copy in sends:
+        copy.wait_send()
+    for copy in local:
+        copy.wait()
+
+
+def exchanged(tiles, hidden, n, groups):
+    _, tall, deep = tiles.shape
+    size = hidden.shape[2]
+    hops = groups // PAIR
+    dma = pltpu.SemaphoreType.DMA
+    return pl.pallas_call(
+        functools.partial(exchange_kernel, n, groups),
+        out_shape=(
+            jax.ShapeDtypeStruct((tall, groups * deep), BF16),
+            jax.ShapeDtypeStruct((groups, deep, size), BF16),
+        ),
+        in_specs=[pl.BlockSpec(memory_space=pl.ANY)] * 2,
+        out_specs=(pl.BlockSpec(memory_space=pl.ANY),) * 2,
+        scratch_shapes=[
+            dma((2, 2)),
+            dma((2, 2, hops)),
+            dma((2, 2, hops)),
+            dma((2, 2, hops, TEAM)),
+            dma((2,)),
+        ],
+        compiler_params=pltpu.CompilerParams(collective_id=1, has_side_effects=True),
+    )(tiles, hidden)
+
+
+def moment_kernel(count_ref, columns_ref, rows_ref, momentum_ref, out_ref, kept):
+    group = lax.axis_index("dp")
+    groups, deep, size = rows_ref.shape
+
+    @pl.when(pl.program_id(0) == 0)
+    def _():
+        at = lax.broadcasted_iota(jnp.int32, (deep, size), 0)
+        for source in range(groups):
+            tallied = at < count_ref[source, group] * TILE
+            values = jnp.where(tallied, rows_ref[source].astype(jnp.float32), 0.0)
+            kept[source * deep : (source + 1) * deep] = values.astype(BF16)
+
+    gradient = dot16(columns_ref[...], kept[...])
+    out_ref[...] = MOMENTUM_DECAY * momentum_ref[...] + gradient
+
+
+def moment_of(counts, columns, rows, momentum):
+    tall, size = momentum.shape
+    stride = math.gcd(tall, 128)
+    return pl.pallas_call(
+        moment_kernel,
+        grid=(tall // stride,),
+        out_shape=jax.ShapeDtypeStruct(momentum.shape, jnp.float32),
+        in_specs=[
+            pl.BlockSpec(memory_space=pltpu.SMEM),
+            pl.BlockSpec((stride, columns.shape[1]), lambda i: (i, 0)),
+            pl.BlockSpec(rows.shape, lambda i: (0, 0, 0)),
+            pl.BlockSpec((stride, size), lambda i: (i, 0)),
+        ],
+        out_specs=pl.BlockSpec((stride, size), lambda i: (i, 0)),
+        scratch_shapes=[pltpu.VMEM((columns.shape[1], size), BF16)],
+        compiler_params=pltpu.CompilerParams(vmem_limit_bytes=56 * 2**20),
+    )(counts, columns, rows, momentum)
+
+
+def widen_kernel(code_ref, top_ref, out_ref):
+    for i in range(code_ref.shape[1]):
+        stride = code_ref.shape[2]
+        rows = slice(i * stride, (i + 1) * stride)
+        out_ref[0, rows] = code_ref[0, i].astype(jnp.float32) * top_ref[0, i : i + 1]
+
+
+def widened(code, top):
+    groups, parts, stride, size = code.shape
+    return pl.pallas_call(
+        widen_kernel,
+        grid=(groups,),
+        out_shape=jax.ShapeDtypeStruct((groups, parts * stride, size), jnp.float32),
+        in_specs=[
+            pl.BlockSpec((1, parts, stride, size), lambda i: (i, 0, 0, 0)),
+            pl.BlockSpec((1, top.shape[1], size), lambda i: (i, 0, 0)),
+        ],
+        out_specs=pl.BlockSpec((1, parts * stride, size), lambda i: (i, 0, 0)),
+        compiler_params=pltpu.CompilerParams(vmem_limit_bytes=56 * 2**20),
+    )(code, top)
 
 
 def iterate_kernel(
@@ -197,37 +369,37 @@
     def strips(step):
         @pl.loop(0, blocks)
         def _(i):
-            step(pl.ds(pl.multiple_of(i * BLOCK, BLOCK), BLOCK))
-
-    def scaled(rows):
-        value = gram[rows] * (factor * factor)
-        gram[rows] = value
-        gram16[rows] = value.astype(BF16)
-
-    def mix_first(rows):
-        value = COEF_B * gram[rows] + COEF_C * dot16(gram16[rows], gram16[...])
-        first[rows] = value
-        first16[rows] = value.astype(BF16)
-
-    def mix_square(rows):
-        value = 2.0 * COEF_A * first[rows] + dot16(first16[rows], first16[...])
-        other[rows] = value.astype(BF16)
-
-    def next_gram(rows):
-        value = COEF_A * COEF_A * gram[rows] + dot16(gram16[rows], other[...])
-        gram[rows] = value
-        mix[rows] = value.astype(BF16)
-
-    def mix_second(rows):
-        value = COEF_B * gram[rows] + COEF_C * dot16(mix[rows], mix[...])
-        gram[rows] = value
-        second16[rows] = value.astype(BF16)
-
-    def mix_both(rows):
-        value = COEF_A * (first[rows] + gram[rows]) + dot16(first16[rows], second16[...])
+            step((slice(None), pl.ds(pl.multiple_of(i * BLOCK, BLOCK), BLOCK)))
+
+    def scaled(cols):
+        value = gram[cols] * (factor * factor)
+        gram[cols] = value
+        gram16[cols] = value.astype(BF16)
+
+    def mix_first(cols):
+        value = COEF_B * gram[cols] + COEF_C * dot16(gram16[...], gram16[cols])
+        first[cols] = value
+        first16[cols] = value.astype(BF16)
+
+    def mix_square(cols):
+        value = 2.0 * COEF_A * first[cols] + dot16(first16[...], first16[cols])
+        other[cols] = value.astype(BF16)
+
+    def next_gram(cols):
+        value = COEF_A * COEF_A * gram[cols] + dot16(gram16[...], other[cols])
+        gram[cols] = value
+        mix[cols] = value.astype(BF16)
+
+    def mix_second(cols):
+        value = COEF_B * gram[cols] + COEF_C * dot16(mix[...], mix[cols])
+        gram[cols] = value
+        second16[cols] = value.astype(BF16)
+
+    def mix_both(cols):
+        value = COEF_A * (first[cols] + gram[cols]) + dot16(first16[...], second16[cols])
         top = value.astype(BF16)
-        gram16[rows] = top
-        mix_low[rows] = (value - top.astype(jnp.float32)).astype(BF16)
+        gram16[cols] = top
+        mix_low[cols] = (value - top.astype(jnp.float32)).astype(BF16)
 
     for step in (scaled, mix_first, mix_square, next_gram, mix_second, mix_both):
         strips(step)
@@ -340,25 +512,16 @@
             collective_id=0, has_side_effects=True, vmem_limit_bytes=56 * 2**20
         ),
     )(moment)
-    update = code.astype(jnp.float32) * top[:, :parts, None]
-    return update.reshape(groups, tall, size)
+    return widened(code, top)
 
 
 def body(hidden_token_tiles, gradient_token_tiles, momentum, filled_tile_count):
-    group = lax.axis_index("dp")
-    rows_group = hidden_token_tiles.shape[1]
-    experts_here = hidden_token_tiles.shape[0]
-    limits = lax.dynamic_index_in_dim(filled_tile_count, group, 0, keepdims=False) * TILE
-    positions = lax.broadcasted_iota(jnp.int32, (experts_here, rows_group), 1)
-    tallied_tiles = positions < limits[:, None]
-    retained_entries = jnp.where(
-        tallied_tiles[:, :, None], hidden_token_tiles, jnp.zeros((), jnp.bfloat16)
+    groups = lax.axis_size("dp")
+    columns_all, rows_all = exchanged(
+        gradient_token_tiles, hidden_token_tiles, lax.axis_size("expert"), groups
     )
-    rows_all = lax.all_to_all(retained_entries, "dp", 0, 1, tiled=True)[0]
-    columns_all = lax.all_to_all(gradient_token_tiles, "dp", 0, 2, tiled=True)[0]
-    gradient = jnp.dot(columns_all, rows_all, preferred_element_type=jnp.float32)
-    moment = MOMENTUM_DECAY * momentum[0] + gradient
-    update = iterated(moment, lax.axis_size("expert"), lax.axis_size("dp"))
+    moment = moment_of(filled_tile_count, columns_all, rows_all, momentum[0])
+    update = iterated(moment, lax.axis_size("expert"), groups)
     return (moment[None], update)
 
 

time: 159 us -> 142 us (0.89)
  Pallas kernels: 105 us -> 141 us
  blocking collectives: 16.9 us -> 0 us
  other arithmetic: 12.1 us -> 0 us
  waiting for transfers between devices: 12.1 us -> 0 us
  matrix products: 5.06 us -> 0 us
  starting transfers between devices: 4.24 us -> 0 us
  local copies, waits for them, and re-layouts: 2.31 us -> 0 us
    pallas_call x0 -> x3, Pallas kernels: none -> 35.2 us  [the longest x1 18.3 us: exchanged(): pl.pallas_call(functools.partial(exchange_kernel, n, groups), out_shape=(...]
    all_to_all x1 -> x0, blocking collectives: 16.9 us -> none  [body(): rows_all = lax.all_to_all(retained_entries, 'dp', 0, 1, tiled=True)[0]]
    all_to_all x1 -> x0, waiting for transfers between devices: 12.1 us -> none  [body(): lax.all_to_all(gradient_token_tiles, 'dp', 0, 2, tiled=True)[0]]
    mul x2 -> x0, other arithmetic: 11.9 us -> none  [the longest x1 11.2 us: iterated(): update = code.astype(jnp.float32) * top[:, :parts, None]]
    dot_general x1 -> x0, matrix products: 5.06 us -> none  [body(): jnp.dot(columns_all, rows_all, preferred_element_type=jnp.float32)]
    all_to_all x1 -> x0, starting transfers between devices: 4.24 us -> none  [body(): lax.all_to_all(gradient_token_tiles, 'dp', 0, 2, tiled=True)[0]]
    unnamed x3 -> x0, local copies, waits for them, and re-layouts: 2.31 us -> none
  transfers between devices with their start and end apart: 1 -> 0, of which waited for: 1 -> 0; matrix products, arithmetic and copies ran while one was open for 1% -> 0% of each run, Pallas kernels for 0% -> 0%
where the time goes in v4:
time: 142 us
  Pallas kernels  141 us (99%)
    pallas_call x1, Pallas kernels, iterated(): pl.pallas_call(functools.partial(iterate_kernel, n, groups, math.sqrt(max...  106 us
    pallas_call x1, Pallas kernels, exchanged(): pl.pallas_call(functools.partial(exchange_kernel, n, groups), out_shape=(...  18.3 us
    pallas_call x1, Pallas kernels, widened(): pl.pallas_call(widen_kernel, grid=(groups,), out_shape=jax.ShapeDtypeStru...  9.04 us
    pallas_call x1, Pallas kernels, moment_of(): pl.pallas_call(moment_kernel, grid=(tall // stride,), out_shape=jax.Shape...  7.88 us

profile of v4, /device:TPU:0, one launch (start us, length us, event | category | flops | bytes accessed | tf_op | source)
XLA Modules:
  0.0 141.8 jit_solution(7214877584816037715)
XLA Ops:
  0.6 18.3 %shard_map.59 = (bf16[896,512]{1,0:T(8,128)(2,1)}, bf16[4,128,1024]{2,1,0:T(8,128)(2,1)}) custom-call(bf16[4,896,128]{2,1,0:T(8,128)(2,1)} %tiles_ref.1, bf16[4,128,1024]{2,1,0:T(8,128)(2,1)} %hidden_ref.1), custom_call_target="tpu_custom_call" | custom-call | tf_op jit(solution)/shard_map/pallas_call | solution.py:137
  18.9 7.9 %shard_map.60.moment_ref = f32[896,1024]{1,0:T(8,128)} custom-call(s32[4,4]{1,0:T(4,128)} %count_ref.1, bf16[896,512]{1,0:T(8,128)(2,1)} %get-tuple-element.6.columns_ref, bf16[4,128,1024]{2,1,0:T(8,128)(2,1)} %get-tuple-element.7.rows_ref, f32[896,1024]{1,0:T(8,128)} %bitcast.3), custom_call_target="tpu_custom_call" | custom-call | tf_op jit(solution)/shard_map/pallas_call | solution.py:175
  26.8 106.0 %shard_map.61 = (s16[4,7,128,1024]{3,2,1,0:T(8,128)(2,1)}, f32[4,8,1024]{2,1,0:T(8,128)}) custom-call(f32[896,1024]{1,0:T(8,128)} %shard_map.60.moment_ref), custom_call_target="tpu_custom_call" | custom-call | tf_op jit(solution)/shard_map/pallas_call | solution.py:502
  132.8 9.0 %shard_map.62 = f32[4,896,1024]{2,1,0:T(8,128)} custom-call(s16[4,7,128,1024]{3,2,1,0:T(8,128)(2,1)} %get-tuple-element.8.code_ref, f32[4,8,1024]{2,1,0:T(8,128)} %get-tuple-element.9.top_ref), custom_call_target="tpu_custom_call" | custom-call | tf_op jit(solution)/shard_map/pallas_call | solution.py:200

commit v5 on v4

--- a/solution.py
+++ b/solution.py
@@ -171,7 +171,7 @@
 
 def moment_of(counts, columns, rows, momentum):
     tall, size = momentum.shape
-    stride = math.gcd(tall, 128)
+    stride = tall // 2
     return pl.pallas_call(
         moment_kernel,
         grid=(tall // stride,),
@@ -327,17 +327,19 @@
     at = 0
     for i in range(blocks):
         rows = slice(i * BLOCK, (i + 1) * BLOCK)
-        rest = slice(i * BLOCK, size)
-        strip = across(high[:, rows], high[:, rest])
-        strip += across(high[:, rows], low[:, rest]) + across(low[:, rows], high[:, rest])
-        for j in range(i, blocks):
-            block = strip[:, (j - i) * BLOCK : (j - i + 1) * BLOCK]
-            work[at // PAIR, at % PAIR] = block.astype(BF16)
-            at += 1
-        if i == 0:
-            pl.semaphore_wait(barrier, places + groups - 1)
-        for chunk in range(len(near_copies), at // PAIR):
-            send_near(chunk)
+        for start in range(i, blocks, PAIR):
+            stop = min(start + PAIR, blocks)
+            rest = slice(start * BLOCK, stop * BLOCK)
+            strip = across(high[:, rows], high[:, rest])
+            strip += across(high[:, rows], low[:, rest]) + across(low[:, rows], high[:, rest])
+            for j in range(start, stop):
+                block = strip[:, (j - start) * BLOCK : (j - start + 1) * BLOCK]
+                work[at // PAIR, at % PAIR] = block.astype(BF16)
+                at += 1
+            if i == start == 0:
+                pl.semaphore_wait(barrier, places + groups - 1)
+            for chunk in range(len(near_copies), at // PAIR):
+                send_near(chunk)
     for step in range(CHUNKS + 2):
         if step < CHUNKS:
             send_far(step)
@@ -358,23 +360,24 @@
     row_at = lax.broadcasted_iota(jnp.int32, (BLOCK, BLOCK), 0)
     col_at = lax.broadcasted_iota(jnp.int32, (BLOCK, BLOCK), 1)
     for at, (i, j) in enumerate(pairs):
-        block = full[at // PAIR, at % PAIR].astype(jnp.float32)
         if i == j:
+            block = full[at // PAIR, at % PAIR].astype(jnp.float32)
             trace += jnp.sum(jnp.where(row_at == col_at, block, 0.0), keepdims=True)
-        gram[i * BLOCK : (i + 1) * BLOCK, j * BLOCK : (j + 1) * BLOCK] = block
+    factor = 1.0 / (jnp.sqrt(trace) + EPSILON)
+    for at, (i, j) in enumerate(pairs):
+        block = full[at // PAIR, at % PAIR].astype(jnp.float32) * (factor * factor)
+        here = (slice(i * BLOCK, (i + 1) * BLOCK), slice(j * BLOCK, (j + 1) * BLOCK))
+        gram[here] = block
+        gram16[here] = block.astype(BF16)
         if i != j:
-            gram[j * BLOCK : (j + 1) * BLOCK, i * BLOCK : (i + 1) * BLOCK] = block.T
-    factor = 1.0 / (jnp.sqrt(trace) + EPSILON)
+            flipped = block.T
+            gram[here[::-1]] = flipped
+            gram16[here[::-1]] = flipped.astype(BF16)
 
     def strips(step):
         @pl.loop(0, blocks)
         def _(i):
             step((slice(None), pl.ds(pl.multiple_of(i * BLOCK, BLOCK), BLOCK)))
-
-    def scaled(cols):
-        value = gram[cols] * (factor * factor)
-        gram[cols] = value
-        gram16[cols] = value.astype(BF16)
 
     def mix_first(cols):
         value = COEF_B * gram[cols] + COEF_C * dot16(gram16[...], gram16[cols])
@@ -401,7 +404,7 @@
         gram16[cols] = top
         mix_low[cols] = (value - top.astype(jnp.float32)).astype(BF16)
 
-    for step in (scaled, mix_first, mix_square, next_gram, mix_second, mix_both):
+    for step in (mix_first, mix_square, next_gram, mix_second, mix_both):
         strips(step)
 
     stride = code.shape[1]

time: 142 us -> 139 us (0.979)
  Pallas kernels: 141 us -> 138 us
    pallas_call x1, Pallas kernels: 7.88 us -> 4.72 us  [moment_of(): pl.pallas_call(moment_kernel, grid=(tall // stride,), out_shape=jax.Shape...]
where the time goes in v5:
time: 139 us
  Pallas kernels  138 us (99%)
    pallas_call x1, Pallas kernels, iterated(): pl.pallas_call(functools.partial(iterate_kernel, n, groups, math.sqrt(max...  106 us
    pallas_call x1, Pallas kernels, exchanged(): pl.pallas_call(functools.partial(exchange_kernel, n, groups), out_shape=(...  18.3 us
    pallas_call x1, Pallas kernels, widened(): pl.pallas_call(widen_kernel, grid=(groups,), out_shape=jax.ShapeDtypeStru...  9.04 us
    pallas_call x1, Pallas kernels, moment_of(): pl.pallas_call(moment_kernel, grid=(tall // stride,), out_shape=jax.Shape...  4.72 us

profile of v5, /device:TPU:0, one launch (start us, length us, event | category | flops | bytes accessed | tf_op | source)
XLA Modules:
  0.0 138.6 jit_solution(9748433855275825875)
XLA Ops:
  0.6 18.3 %shard_map.59 = (bf16[896,512]{1,0:T(8,128)(2,1)}, bf16[4,128,1024]{2,1,0:T(8,128)(2,1)}) custom-call(bf16[4,896,128]{2,1,0:T(8,128)(2,1)} %tiles_ref.1, bf16[4,128,1024]{2,1,0:T(8,128)(2,1)} %hidden_ref.1), custom_call_target="tpu_custom_call" | custom-call | tf_op jit(solution)/shard_map/pallas_call | solution.py:137
  18.9 4.7 %shard_map.60.moment_ref = f32[896,1024]{1,0:T(8,128)} custom-call(s32[4,4]{1,0:T(4,128)} %count_ref.1, bf16[896,512]{1,0:T(8,128)(2,1)} %get-tuple-element.6.columns_ref, bf16[4,128,1024]{2,1,0:T(8,128)(2,1)} %get-tuple-element.7.rows_ref, f32[896,1024]{1,0:T(8,128)} %bitcast.3), custom_call_target="tpu_custom_call" | custom-call | tf_op jit(solution)/shard_map/pallas_call | solution.py:175
  23.6 105.9 %shard_map.61 = (s16[4,7,128,1024]{3,2,1,0:T(8,128)(2,1)}, f32[4,8,1024]{2,1,0:T(8,128)}) custom-call(f32[896,1024]{1,0:T(8,128)} %shard_map.60.moment_ref), custom_call_target="tpu_custom_call" | custom-call | tf_op jit(solution)/shard_map/pallas_call | solution.py:505
  129.6 9.0 %shard_map.62 = f32[4,896,1024]{2,1,0:T(8,128)} custom-call(s16[4,7,128,1024]{3,2,1,0:T(8,128)(2,1)} %get-tuple-element.8.code_ref, f32[4,8,1024]{2,1,0:T(8,128)} %get-tuple-element.9.top_ref), custom_call_target="tpu_custom_call" | custom-call | tf_op jit(solution)/shard_map/pallas_call | solution.py:200
